TPU v7x, 256 devices: a whole 4x4x8 slice. The times are simulated.
256 devices in a mesh: grp: 32 (over y_lo, z, core), blk: 8 (over y_hi, x).
Axes of the slice: x: 4, y: 4 (y_hi: 2, y_lo: 2; y = y_hi * 2 + y_lo), z: 8, core: 2. Of those that a mesh axis runs over, the one named last changes fastest.
Arguments:
- tiles: bfloat16 [16384, 16384], P(('blk', 'grp'))
- exponents: int32 [256, 256], P(('blk', 'grp')), may hold values from -2 to 2, as said below
- rhs: bfloat16 [32, 16384], P(None, ('blk', 'grp'))
- elem_frac: int32 [16384], P(('blk', 'grp')), may hold values from 0 to 63
- compliance: float32 [64], replicated, may hold values from 0.3 to 1.5
- scen_map: int32 [32], replicated, may hold values from 0 to 31, each once
Outputs:
- basis: bfloat16 [32, 16384], P(None, ('blk', 'grp'))
- root_mean: float32 [12, 32], replicated
Inputs may be any that keep to these rules, and one draw needn't show every extreme that they name: Integer tile exponents. `scen_map`: each scenario row taken once.
All inputs are finite; a program needn't handle non-finite values.
Results may differ from a plain program's by a relative error of at most 0.014.
Values may be sent and summed in bfloat16 or wider, within the bound.
A program may use at most 64 MiB of HBM per device.

v0:
```python
import jax
import jax.numpy as jnp
from jax import lax
from jax.sharding import PartitionSpec as P

STEPS = 12


def on_device(tiles, exponents, rhs, elem_frac, compliance, scen_map):
    tile_rows = tiles.shape[0]
    all_elems = tiles.shape[1]
    scen_count = rhs.shape[0]
    scen_pick = (scen_map[None, :] == jnp.arange(scen_count, dtype=jnp.int32)[:, None]).astype(
        jnp.bfloat16
    )
    basis = jnp.dot(scen_pick.T, rhs, preferred_element_type=jnp.float32).astype(jnp.bfloat16)
    membership = (
        elem_frac[:, None] == jnp.arange(compliance.shape[0], dtype=jnp.int32)[None, :]
    ).astype(jnp.float32)
    local_diag = jnp.dot(membership, compliance, precision=lax.Precision.HIGHEST)
    tile_scale = jnp.exp2(exponents[0].astype(jnp.float32))
    cycle_size = lax.axis_size("blk")
    group_size = lax.axis_size("grp")
    history = []
    for iteration in range(STEPS):
        beside_all = lax.all_gather(basis, "blk", axis=1, tiled=True)
        tile_grid = tiles.reshape(tile_rows, cycle_size, group_size, tile_rows)
        gain_grid = tile_scale.reshape(cycle_size, group_size)
        piece = lax.all_gather(beside_all, "grp", axis=1, tiled=True)
        shard_count = piece.shape[1] // (cycle_size * tile_rows)
        partial_value = jnp.einsum(
            "rbgc,sgbc->srbg",
            tile_grid,
            piece.reshape(scen_count, shard_count, cycle_size, tile_rows),
            preferred_element_type=jnp.float32,
        )
        product = jnp.sum(partial_value * gain_grid[None, None], axis=(2, 3))
        image = product + local_diag[None, :] * basis.astype(jnp.float32)
        squares = lax.psum(jnp.sum(image * image, axis=1), ("grp", "blk"))
        root_mean = jnp.sqrt(squares / all_elems + 1e-06)
        history.append(root_mean)
        basis = (image / root_mean[:, None]).astype(jnp.bfloat16)
    return (basis, jnp.stack(history))


def solution(mesh):
    placed = (
        P(("blk", "grp"), None),
        P(("blk", "grp"), None),
        P(None, ("blk", "grp")),
        P(("blk", "grp")),
        P(),
        P(),
    )
    return jax.shard_map(
        on_device,
        mesh=mesh,
        in_specs=placed,
        out_specs=(P(None, ("blk", "grp")), P()),
        check_vma=False,
    )
```

profile of v0, /device:TPU:1, one launch (start us, length us, event | category | flops | bytes accessed | tf_op | source)
XLA Modules:
  0.0 2205.5 jit_solution(7111363562382377715)
XLA Ops:
  8.7 29.2 %all-gather = bf16[8,64,32]{1,2,0:T(8,128)(2,1)S(1)} all-gather(bf16[1,64,32]{1,2,0:T(8,128)(2,1)S(1)} %bitcast.114), channel_id=1, replica_groups=mesh['grp'=32,'blk'=8] {'blk'}, dimensions={0}, use_global_device_ids=true | all-gather | bytes 36864 | tf_op jit(solution)/shard_map/all_gather | solution.py:26
  46.2 65.2 %all-gather.25.cloned.1.call-done = bf16[32,16384]{1,0:T(8,128)(2,1)} async-done(((bf16[32,512]{1,0:T(8,128)(2,1)}), bf16[32,16384]{1,0:T(8,128)(2,1)}) %all-gather.25.cloned.1.call-update) | async-done | bytes 1048592 | tf_op jit(solution)/shard_map/all_gather | solution.py:29
  121.8 75.6 %psum.84 = f32[32]{0:T(128)S(1)} all-reduce(f32[32]{0:T(128)S(1)} %multiply_reduce_fusion.23), channel_id=1, replica_groups=mesh['grp'=32,'blk'=8] {'grp','blk'}, use_global_device_ids=true, to_apply=%region_2.0 | all-reduce | flops 32 | bytes 256 | tf_op jit(solution)/shard_map/psum | solution.py:39
  226.6 66.4 %all-gather.27.cloned.1.call-done = bf16[32,16384]{1,0:T(8,128)(2,1)} async-done(((bf16[32,512]{1,0:T(8,128)(2,1)}), bf16[32,16384]{1,0:T(8,128)(2,1)}) %all-gather.27.cloned.1.call-update) | async-done | bytes 1048592 | tf_op jit(solution)/shard_map/all_gather | solution.py:29
  303.5 75.6 %psum.85 = f32[32]{0:T(128)S(1)} all-reduce(f32[32]{0:T(128)S(1)} %multiply_reduce_fusion.22), channel_id=1, replica_groups=mesh['grp'=32,'blk'=8] {'grp','blk'}, use_global_device_ids=true, to_apply=%region_5.0 | all-reduce | flops 32 | bytes 256 | tf_op jit(solution)/shard_map/psum | solution.py:39
  379.2 28.1 %all-gather.2 = bf16[8,64,32]{1,2,0:T(8,128)(2,1)S(1)} all-gather(bf16[1,64,32]{1,2,0:T(8,128)(2,1)S(1)} %bitcast.117), channel_id=1, replica_groups=mesh['grp'=32,'blk'=8] {'blk'}, dimensions={0}, use_global_device_ids=true | all-gather | bytes 36864 | tf_op jit(solution)/shard_map/all_gather | solution.py:26
  408.4 66.4 %all-gather.29.cloned.1.call-done = bf16[32,16384]{1,0:T(8,128)(2,1)} async-done(((bf16[32,512]{1,0:T(8,128)(2,1)}), bf16[32,16384]{1,0:T(8,128)(2,1)}) %all-gather.29.cloned.1.call-update) | async-done | bytes 1048592 | tf_op jit(solution)/shard_map/all_gather | solution.py:29
  485.2 75.6 %psum.86 = f32[32]{0:T(128)S(1)} all-reduce(f32[32]{0:T(128)S(1)} %multiply_reduce_fusion.21), channel_id=1, replica_groups=mesh['grp'=32,'blk'=8] {'grp','blk'}, use_global_device_ids=true, to_apply=%region_8.0 | all-reduce | flops 32 | bytes 256 | tf_op jit(solution)/shard_map/psum | solution.py:39
  560.9 28.1 %all-gather.3 = bf16[8,64,32]{1,2,0:T(8,128)(2,1)S(1)} all-gather(bf16[1,64,32]{1,2,0:T(8,128)(2,1)S(1)} %bitcast.118), channel_id=1, replica_groups=mesh['grp'=32,'blk'=8] {'blk'}, dimensions={0}, use_global_device_ids=true | all-gather | bytes 36864 | tf_op jit(solution)/shard_map/all_gather | solution.py:26
  590.3 66.1 %all-gather.31.cloned.1.call-done = bf16[32,16384]{1,0:T(8,128)(2,1)} async-done(((bf16[32,512]{1,0:T(8,128)(2,1)}), bf16[32,16384]{1,0:T(8,128)(2,1)}) %all-gather.31.cloned.1.call-update) | async-done | bytes 1048592 | tf_op jit(solution)/shard_map/all_gather | solution.py:29
  666.9 75.6 %psum.87 = f32[32]{0:T(128)S(1)} all-reduce(f32[32]{0:T(128)S(1)} %multiply_reduce_fusion.20), channel_id=1, replica_groups=mesh['grp'=32,'blk'=8] {'grp','blk'}, use_global_device_ids=true, to_apply=%region_11.0 | all-reduce | flops 32 | bytes 256 | tf_op jit(solution)/shard_map/psum | solution.py:39
  771.6 66.4 %all-gather.33.cloned.1.call-done = bf16[32,16384]{1,0:T(8,128)(2,1)} async-done(((bf16[32,512]{1,0:T(8,128)(2,1)}), bf16[32,16384]{1,0:T(8,128)(2,1)}) %all-gather.33.cloned.1.call-update) | async-done | bytes 1048592 | tf_op jit(solution)/shard_map/all_gather | solution.py:29
  848.5 75.6 %psum.88 = f32[32]{0:T(128)S(1)} all-reduce(f32[32]{0:T(128)S(1)} %multiply_reduce_fusion.19), channel_id=1, replica_groups=mesh['grp'=32,'blk'=8] {'grp','blk'}, use_global_device_ids=true, to_apply=%region_14.0 | all-reduce | flops 32 | bytes 256 | tf_op jit(solution)/shard_map/psum | solution.py:39
  924.3 28.1 %all-gather.5 = bf16[8,64,32]{1,2,0:T(8,128)(2,1)S(1)} all-gather(bf16[1,64,32]{1,2,0:T(8,128)(2,1)S(1)} %bitcast.120), channel_id=1, replica_groups=mesh['grp'=32,'blk'=8] {'blk'}, dimensions={0}, use_global_device_ids=true | all-gather | bytes 36864 | tf_op jit(solution)/shard_map/all_gather | solution.py:26
  953.4 66.4 %all-gather.35.cloned.1.call-done = bf16[32,16384]{1,0:T(8,128)(2,1)} async-done(((bf16[32,512]{1,0:T(8,128)(2,1)}), bf16[32,16384]{1,0:T(8,128)(2,1)}) %all-gather.35.cloned.1.call-update) | async-done | bytes 1048592 | tf_op jit(solution)/shard_map/all_gather | solution.py:29
  1030.2 75.6 %psum.89 = f32[32]{0:T(128)S(1)} all-reduce(f32[32]{0:T(128)S(1)} %multiply_reduce_fusion.18), channel_id=1, replica_groups=mesh['grp'=32,'blk'=8] {'grp','blk'}, use_global_device_ids=true, to_apply=%region_17.0 | all-reduce | flops 32 | bytes 256 | tf_op jit(solution)/shard_map/psum | solution.py:39
  1106.0 28.1 %all-gather.6 = bf16[8,64,32]{1,2,0:T(8,128)(2,1)S(1)} all-gather(bf16[1,64,32]{1,2,0:T(8,128)(2,1)S(1)} %bitcast.121), channel_id=1, replica_groups=mesh['grp'=32,'blk'=8] {'blk'}, dimensions={0}, use_global_device_ids=true | all-gather | bytes 36864 | tf_op jit(solution)/shard_map/all_gather | solution.py:26
  1135.1 66.4 %all-gather.37.cloned.1.call-done = bf16[32,16384]{1,0:T(8,128)(2,1)} async-done(((bf16[32,512]{1,0:T(8,128)(2,1)}), bf16[32,16384]{1,0:T(8,128)(2,1)}) %all-gather.37.cloned.1.call-update) | async-done | bytes 1048592 | tf_op jit(solution)/shard_map/all_gather | solution.py:29
  1211.9 75.6 %psum.90 = f32[32]{0:T(128)S(1)} all-reduce(f32[32]{0:T(128)S(1)} %multiply_reduce_fusion.17), channel_id=1, replica_groups=mesh['grp'=32,'blk'=8] {'grp','blk'}, use_global_device_ids=true, to_apply=%region_20.0 | all-reduce | flops 32 | bytes 256 | tf_op jit(solution)/shard_map/psum | solution.py:39
  1317.0 66.1 %all-gather.39.cloned.1.call-done = bf16[32,16384]{1,0:T(8,128)(2,1)} async-done(((bf16[32,512]{1,0:T(8,128)(2,1)}), bf16[32,16384]{1,0:T(8,128)(2,1)}) %all-gather.39.cloned.1.call-update) | async-done | bytes 1048592 | tf_op jit(solution)/shard_map/all_gather | solution.py:29
  1393.6 75.6 %psum.91 = f32[32]{0:T(128)S(1)} all-reduce(f32[32]{0:T(128)S(1)} %multiply_reduce_fusion.16), channel_id=1, replica_groups=mesh['grp'=32,'blk'=8] {'grp','blk'}, use_global_device_ids=true, to_apply=%region_23.0 | all-reduce | flops 32 | bytes 256 | tf_op jit(solution)/shard_map/psum | solution.py:39
  1469.3 28.1 %all-gather.8 = bf16[8,64,32]{1,2,0:T(8,128)(2,1)S(1)} all-gather(bf16[1,64,32]{1,2,0:T(8,128)(2,1)S(1)} %bitcast.123), channel_id=1, replica_groups=mesh['grp'=32,'blk'=8] {'blk'}, dimensions={0}, use_global_device_ids=true | all-gather | bytes 36864 | tf_op jit(solution)/shard_map/all_gather | solution.py:26
  1498.4 66.4 %all-gather.41.cloned.1.call-done = bf16[32,16384]{1,0:T(8,128)(2,1)} async-done(((bf16[32,512]{1,0:T(8,128)(2,1)}), bf16[32,16384]{1,0:T(8,128)(2,1)}) %all-gather.41.cloned.1.call-update) | async-done | bytes 1048592 | tf_op jit(solution)/shard_map/all_gather | solution.py:29
  1575.3 75.6 %psum.92 = f32[32]{0:T(128)S(1)} all-reduce(f32[32]{0:T(128)S(1)} %multiply_reduce_fusion.15), channel_id=1, replica_groups=mesh['grp'=32,'blk'=8] {'grp','blk'}, use_global_device_ids=true, to_apply=%region_26.0 | all-reduce | flops 32 | bytes 256 | tf_op jit(solution)/shard_map/psum | solution.py:39
  1651.0 28.1 %all-gather.9 = bf16[8,64,32]{1,2,0:T(8,128)(2,1)S(1)} all-gather(bf16[1,64,32]{1,2,0:T(8,128)(2,1)S(1)} %bitcast.124), channel_id=1, replica_groups=mesh['grp'=32,'blk'=8] {'blk'}, dimensions={0}, use_global_device_ids=true | all-gather | bytes 36864 | tf_op jit(solution)/shard_map/all_gather | solution.py:26
  1680.1 66.4 %all-gather.43.cloned.1.call-done = bf16[32,16384]{1,0:T(8,128)(2,1)} async-done(((bf16[32,512]{1,0:T(8,128)(2,1)}), bf16[32,16384]{1,0:T(8,128)(2,1)}) %all-gather.43.cloned.1.call-update) | async-done | bytes 1048592 | tf_op jit(solution)/shard_map/all_gather | solution.py:29
  1757.0 75.6 %psum.93 = f32[32]{0:T(128)S(1)} all-reduce(f32[32]{0:T(128)S(1)} %multiply_reduce_fusion.14), channel_id=1, replica_groups=mesh['grp'=32,'blk'=8] {'grp','blk'}, use_global_device_ids=true, to_apply=%region_29.0 | all-reduce | flops 32 | bytes 256 | tf_op jit(solution)/shard_map/psum | solution.py:39
  1861.8 66.4 %all-gather.45.cloned.1.call-done = bf16[32,16384]{1,0:T(8,128)(2,1)} async-done(((bf16[32,512]{1,0:T(8,128)(2,1)}), bf16[32,16384]{1,0:T(8,128)(2,1)}) %all-gather.45.cloned.1.call-update) | async-done | bytes 1048592 | tf_op jit(solution)/shard_map/all_gather | solution.py:29
  1938.6 75.6 %psum.94 = f32[32]{0:T(128)S(1)} all-reduce(f32[32]{0:T(128)S(1)} %multiply_reduce_fusion.13), channel_id=1, replica_groups=mesh['grp'=32,'blk'=8] {'grp','blk'}, use_global_device_ids=true, to_apply=%region_32.0 | all-reduce | flops 32 | bytes 256 | tf_op jit(solution)/shard_map/psum | solution.py:39
  2014.4 28.4 %all-gather.11 = bf16[8,64,32]{1,2,0:T(8,128)(2,1)S(1)} all-gather(bf16[1,64,32]{1,2,0:T(8,128)(2,1)S(1)} %bitcast.115), channel_id=1, replica_groups=mesh['grp'=32,'blk'=8] {'blk'}, dimensions={0}, use_global_device_ids=true | all-gather | bytes 36864 | tf_op jit(solution)/shard_map/all_gather | solution.py:26
  2043.5 66.7 %all-gather.47.cloned.1.call-done = bf16[32,16384]{1,0:T(8,128)(2,1)} async-done(((bf16[32,512]{1,0:T(8,128)(2,1)}), bf16[32,16384]{1,0:T(8,128)(2,1)}) %all-gather.47.cloned.1.call-update) | async-done | bytes 1048592 | tf_op jit(solution)/shard_map/all_gather | solution.py:29
  2120.6 75.6 %psum.95 = f32[32]{0:T(128)S(1)} all-reduce(f32[32]{0:T(128)S(1)} %multiply_reduce_fusion.12), channel_id=1, replica_groups=mesh['grp'=32,'blk'=8] {'grp','blk'}, use_global_device_ids=true, to_apply=%region_35.0 | all-reduce | flops 32 | bytes 256 | tf_op jit(solution)/shard_map/psum | solution.py:39
  (124 shorter events, 261.6 us)
Async XLA Ops:
  7.2 0.7 copy-start
  7.2 38.8 %copy-start.2 = (f32[64]{0:T(128)S(1)}, f32[64]{0:T(128)}, u32[]{:S(2)}) copy-start(f32[64]{0:T(128)} %param.10) | copy-start | bytes 772
  7.2 38.8 %copy-start.1 = (s32[64]{0:T(128)S(1)}, s32[64]{0:T(128)}, u32[]{:S(2)}) copy-start(s32[64]{0:T(128)} %param.9) | copy-start | bytes 772
  7.2 104.2 %all-gather.25.cloned.1.call-start = ((), (), s32[]{:S(2)}) async-start(), calls=%async_computation | async-start | bytes 1081344 | tf_op jit(solution)/shard_map/all_gather | solution.py:29
  38.7 254.4 %all-gather.27.cloned.1.call-start = ((), (), s32[]{:S(2)}) async-start(), calls=%async_computation.1 | async-start | bytes 1081344 | tf_op jit(solution)/shard_map/all_gather | solution.py:29
  226.3 248.4 %all-gather.29.cloned.1.call-start = ((), (), s32[]{:S(2)}) async-start(), calls=%async_computation.2 | async-start | bytes 1081344 | tf_op jit(solution)/shard_map/all_gather | solution.py:29
  408.1 248.3 %all-gather.31.cloned.1.call-start = ((), (), s32[]{:S(2)}) async-start(), calls=%async_computation.3 | async-start | bytes 1081344 | tf_op jit(solution)/shard_map/all_gather | solution.py:29
  589.7 248.3 %all-gather.33.cloned.1.call-start = ((), (), s32[]{:S(2)}) async-start(), calls=%async_computation.4 | async-start | bytes 1081344 | tf_op jit(solution)/shard_map/all_gather | solution.py:29
  771.4 248.3 %all-gather.35.cloned.1.call-start = ((), (), s32[]{:S(2)}) async-start(), calls=%async_computation.5 | async-start | bytes 1081344 | tf_op jit(solution)/shard_map/all_gather | solution.py:29
  953.1 248.3 %all-gather.37.cloned.1.call-start = ((), (), s32[]{:S(2)}) async-start(), calls=%async_computation.6 | async-start | bytes 1081344 | tf_op jit(solution)/shard_map/all_gather | solution.py:29
  1134.8 248.3 %all-gather.39.cloned.1.call-start = ((), (), s32[]{:S(2)}) async-start(), calls=%async_computation.7 | async-start | bytes 1081344 | tf_op jit(solution)/shard_map/all_gather | solution.py:29
  1316.5 248.3 %all-gather.41.cloned.1.call-start = ((), (), s32[]{:S(2)}) async-start(), calls=%async_computation.8 | async-start | bytes 1081344 | tf_op jit(solution)/shard_map/all_gather | solution.py:29
  1498.2 248.3 %all-gather.43.cloned.1.call-start = ((), (), s32[]{:S(2)}) async-start(), calls=%async_computation.9 | async-start | bytes 1081344 | tf_op jit(solution)/shard_map/all_gather | solution.py:29
  1679.8 248.3 %all-gather.45.cloned.1.call-start = ((), (), s32[]{:S(2)}) async-start(), calls=%async_computation.10 | async-start | bytes 1081344 | tf_op jit(solution)/shard_map/all_gather | solution.py:29
  1861.5 248.6 %all-gather.47.cloned.1.call-start = ((), (), s32[]{:S(2)}) async-start(), calls=%async_computation.11 | async-start | bytes 1081344 | tf_op jit(solution)/shard_map/all_gather | solution.py:29
Sparse Core Ops, SparseCore 0:
  38.8 72.5 all-gather.24
  226.5 66.5 all-gather.26
  408.2 66.4 all-gather.28
  589.9 66.4 all-gather.30
  771.5 66.4 all-gather.32
  953.2 66.4 all-gather.34
  1134.9 66.4 all-gather.36
  1316.6 66.4 all-gather.38
  1498.3 66.4 all-gather.40
  1680.0 66.4 all-gather.42
  1861.7 66.4 all-gather.44
  2043.6 66.4 all-gather.46
where the time goes:
time: 2210 us
  blocking collectives  1250 us (57%)
  waiting for transfers between devices  796 us (36%)
  matrix products  88.5 us (4%)
  local copies, waits for them, and re-layouts  53.7 us (2%)
    psum x12, blocking collectives, on_device(): squares = lax.psum(jnp.sum(image * image, axis=1), ('grp', 'blk'))  908 us
    all_gather x12, waiting for transfers between devices, on_device(): piece = lax.all_gather(beside_all, 'grp', axis=1, tiled=True)  795 us
    all_gather x12, blocking collectives, on_device(): beside_all = lax.all_gather(basis, 'blk', axis=1, tiled=True)  338 us
    dot_general x12, matrix products, on_device(): jnp.einsum('rbgc,sgbc->srbg', tile_grid, piece.reshape(scen_count, shard_...  87.5 us
  transfers between devices with their start and end apart: 12, of which 12 were waited for; matrix products, arithmetic and copies ran while one was open for 0% of the time, Pallas kernels for 0%

commit v1 on v0

v1 whole, which is shorter than its diff:
```python
import functools

import jax
import jax.numpy as jnp
from jax import lax
from jax.experimental import pallas as pl
from jax.experimental.pallas import tpu as pltpu
from jax.sharding import PartitionSpec as P

STEPS = 12
NX, NY, NZ = 4, 4, 8
CHIPS = NX * NY * NZ
HALF = 16
ROWS = 128
KEEP = 64
ALL = CHIPS * ROWS
MESH = pl.DeviceIdType.MESH
F32, BF16 = jnp.float32, jnp.bfloat16


def hops(delta):
    return sum(min(d, n - d) for d, n in zip(delta, (NX, NY, NZ)))


DELTAS = sorted(
    [(dx, dy, dz) for dz in range(NZ) for dx in range(NX) for dy in range(NY) if dx or dy or dz],
    key=lambda d: -hops(d),
)


def device(x, y, z, core):
    return {"blk": lax.div(y, 2) * NX + x, "grp": lax.rem(y, 2) * 16 + z * 2 + core}


def iota(shape, dim):
    return lax.broadcasted_iota(jnp.int32, shape, dim)


def as_column(row):
    n = row.shape[1]
    eye = iota((n, n), 0) == iota((n, n), 1)
    return jnp.sum(jnp.where(eye, jnp.broadcast_to(row, (n, n)), 0.0), axis=1, keepdims=True)


def kernel(
    tiles, expo, rhs, frac, comp, smap, basis_out, rms_out,
    amat, vbuf, start, started, diag_mine, diag_other, gains, norms, history, last,
    load_sem, swap_send, swap_recv, send, recv,
):
    blk, grp = lax.axis_index("blk"), lax.axis_index("grp")
    x, y = lax.rem(blk, NX), lax.div(blk, NX) * 2 + lax.div(grp, 16)
    z, core = lax.rem(lax.div(grp, 2), NZ), lax.rem(grp, 2)
    other = 1 - core
    mine = lax.div(y, 2) * 64 + x * 16 + lax.rem(y, 2) * 8 + z
    sibling = device(x, y, z, other)
    peers = [
        device(lax.rem(x + dx, NX), lax.rem(y + dy, NY), lax.rem(z + dz, NZ), core)
        for dx, dy, dz in DELTAS
    ]

    own_rows = pl.ds(pl.multiple_of(core * KEEP, KEEP), KEEP)
    load = pltpu.make_async_copy(tiles, amat.at[own_rows], load_sem)
    load.start()

    barrier = pltpu.get_barrier_semaphore()
    for peer in [sibling, *peers]:
        pl.semaphore_signal(barrier, inc=1, device_id=peer, device_id_type=MESH)

    picked = as_column(smap[...].astype(F32)) == iota((32, 32), 1).astype(F32)
    first = jnp.dot(
        jnp.where(picked, 1.0, 0.0).astype(BF16), rhs[...], preferred_element_type=F32
    )
    first = jnp.concatenate([first, first], axis=1).astype(BF16)
    start[0] = first[:HALF]
    start[1] = first[HALF:]
    member = iota((64, KEEP), 0) == frac[...]
    local_diag = jnp.sum(
        jnp.where(member, as_column(comp[...]), 0.0), axis=0, keepdims=True
    )
    diag_mine[...] = jnp.broadcast_to(
        jnp.concatenate([local_diag, local_diag], axis=1), (8, ROWS)
    )
    scale_row = jnp.exp2(expo[...].astype(F32)).astype(BF16).astype(F32)
    spread = jnp.where(
        (iota((CHIPS, 256), 1) >> 1) == iota((CHIPS, 256), 0), scale_row, 0.0
    ).astype(BF16)
    sides = jnp.where(
        (iota((256, ROWS), 0) & 1) == (iota((256, ROWS), 1) >> 6), 1.0, 0.0
    ).astype(BF16)
    gains[...] = jnp.dot(spread, sides, preferred_element_type=F32)

    pl.semaphore_wait(barrier, 1 + len(peers))

    def swap(src, dst, i):
        return pltpu.make_async_remote_copy(
            src, dst, swap_send.at[i], swap_recv.at[i], device_id=sibling, device_id_type=MESH
        )

    swap_start = swap(start.at[other], started, 0)
    swap_start.start()
    swap_diag = swap(diag_mine, diag_other, 1)
    swap_diag.start()

    ours = (iota((1, ROWS), 1) >> 6) == core

    def whole(sem, par):
        part = vbuf.at[par, pl.ds(0, CHIPS - 1)]
        return pltpu.make_async_copy(part, part, sem.at[par])

    def post(par):
        block = vbuf.at[par, mine]
        for peer in peers:
            pltpu.make_async_remote_copy(
                block, block, send.at[par], recv.at[par], device_id=peer, device_id_type=MESH
            ).start()

    swap_start.wait()
    vbuf[0, mine] = jnp.where(ours, start[core], started[...])
    post(0)

    load.wait()

    def scale(b, _):
        gain = jnp.broadcast_to(gains[pl.ds(b, 1), :], (16, ROWS)).astype(BF16)
        columns = pl.ds(pl.multiple_of(b * ROWS, ROWS), ROWS)
        for i in range(KEEP // 16):
            rows = pl.ds(pl.multiple_of(core * KEEP + 16 * i, 16), 16)
            amat[rows, columns] = amat[rows, columns] * gain
        return 0

    lax.fori_loop(0, CHIPS, scale, 0, unroll=4)
    swap_rows = swap(amat.at[own_rows], amat.at[own_rows], 2)
    swap_rows.start()
    swap_diag.wait()
    diag = jnp.where(ours, diag_mine[0:1], diag_other[0:1])
    swap_rows.wait()

    lane = iota((HALF, ROWS), 1)

    def product(step, par):
        whole(recv, par).wait()
        sums = [jnp.zeros((HALF, ROWS), F32) for _ in range(4)]
        for b in range(CHIPS):
            value = vbuf[par, b].astype(F32)
            sums[b % 4] += value * value
        squares = jnp.sum((sums[0] + sums[1]) + (sums[2] + sums[3]), axis=1, keepdims=True)
        root = jnp.sqrt(squares / ALL + 1e-06)
        opening = step == 0
        history[core] = jnp.where(lane == step - 1, root, history[core])
        root = jnp.where(opening, 1.0, root)
        shrink = jnp.exp2(-jnp.floor(jnp.log2(root))).astype(BF16).astype(F32)
        inverse = 1.0 / root
        spread16 = jnp.broadcast_to(shrink, (HALF, ROWS)).astype(BF16)
        total = jnp.zeros((HALF, ROWS), F32)
        group = 16
        for g in range(CHIPS // group):
            part = jnp.concatenate(
                [vbuf[par, g * group + i] * spread16 for i in range(group)], axis=1
            )
            total += lax.dot_general(
                part, amat[:, g * group * ROWS : (g + 1) * group * ROWS],
                (((1,), (1,)), ((), ())), preferred_element_type=F32,
            )
        own = vbuf[par, mine].astype(F32)
        return total * (inverse / shrink) + diag * (own * inverse)

    history[core] = jnp.zeros((HALF, ROWS), F32)

    def advance(step, _):
        par = lax.rem(step, 2)
        image = product(step, par)

        @pl.when(step >= 1)
        def _():
            whole(send, 1 - par).wait()

        vbuf[1 - par, mine] = image.astype(BF16)
        post(1 - par)
        return 0

    lax.fori_loop(0, STEPS - 1, advance, 0)
    image = product(STEPS - 1, (STEPS - 1) % 2)

    eye = iota((HALF, ROWS), 0) == lane
    square = jnp.sum(image * image, axis=1, keepdims=True)
    norms[pl.ds(mine, 1), :] = jnp.sum(jnp.where(eye, square, 0.0), axis=0, keepdims=True)
    whole(send, 0).wait()
    row = norms.at[pl.ds(mine, 1)]
    for peer in peers:
        pltpu.make_async_remote_copy(
            row, row, send.at[0], recv.at[0], device_id=peer, device_id_type=MESH
        ).start()
    rows = norms.at[pl.ds(0, CHIPS - 1)]
    pltpu.make_async_copy(rows, rows, recv.at[0]).wait()
    total = jnp.sum(norms[...], axis=0, keepdims=True)
    squares = jnp.sum(jnp.where(eye, total, 0.0), axis=1, keepdims=True)
    root = jnp.sqrt(squares / ALL + 1e-06)
    history[core] = jnp.where(lane == STEPS - 1, root, history[core])
    last[core] = (image / root).astype(BF16)
    swap_last = swap(last.at[core], last.at[core], 3)
    swap_history = swap(history.at[core], history.at[core], 4)
    swap_last.start()
    swap_history.start()
    pltpu.make_async_copy(rows, rows, send.at[0]).wait()
    whole(send, 1).wait()
    swap_last.wait()
    swap_history.wait()
    result = jnp.concatenate([last[0], last[1]], axis=0).astype(F32)
    basis_out[...] = jnp.where(core == 0, result[:, :KEEP], result[:, KEEP:]).astype(BF16)
    table = jnp.concatenate([history[0], history[1]], axis=0)
    rms_out[...] = table.T[:STEPS]


def on_device(tiles, exponents, rhs, elem_frac, compliance, scen_map):
    vmem = pl.BlockSpec(memory_space=pltpu.VMEM)
    return tuple(
        pl.pallas_call(
            kernel,
            out_shape=(
                jax.ShapeDtypeStruct((32, KEEP), BF16),
                jax.ShapeDtypeStruct((STEPS, 32), F32),
            ),
            in_specs=[pl.BlockSpec(memory_space=pl.ANY)] + [vmem] * 5,
            out_specs=(vmem, vmem),
            scratch_shapes=[
                pltpu.VMEM((ROWS, ALL), BF16),
                pltpu.VMEM((2, CHIPS, HALF, ROWS), BF16),
                pltpu.VMEM((2, HALF, ROWS), BF16),
                pltpu.VMEM((HALF, ROWS), BF16),
                pltpu.VMEM((8, ROWS), F32),
                pltpu.VMEM((8, ROWS), F32),
                pltpu.VMEM((CHIPS, ROWS), F32),
                pltpu.VMEM((CHIPS, ROWS), F32),
                pltpu.VMEM((2, HALF, ROWS), F32),
                pltpu.VMEM((2, HALF, ROWS), BF16),
                pltpu.SemaphoreType.DMA,
                pltpu.SemaphoreType.DMA((5,)),
                pltpu.SemaphoreType.DMA((5,)),
                pltpu.SemaphoreType.DMA((2,)),
                pltpu.SemaphoreType.DMA((2,)),
            ],
            compiler_params=pltpu.CompilerParams(
                collective_id=0, has_side_effects=True, vmem_limit_bytes=32 << 20
            ),
            cost_estimate=pl.CostEstimate(
                flops=2 * STEPS * 32 * KEEP * ALL, bytes_accessed=2 * KEEP * ALL, transcendentals=0
            ),
            name="krylov",
        )(
            tiles,
            exponents,
            rhs,
            elem_frac.reshape(1, KEEP),
            compliance.reshape(1, 64),
            scen_map.reshape(1, 32),
        )
    )


def solution(mesh):
    placed = (
        P(("blk", "grp"), None),
        P(("blk", "grp"), None),
        P(None, ("blk", "grp")),
        P(("blk", "grp")),
        P(),
        P(),
    )
    return jax.shard_map(
        on_device,
        mesh=mesh,
        in_specs=placed,
        out_specs=(P(None, ("blk", "grp")), P()),
        check_vma=False,
    )
```

time: 2210 us -> 216 us (0.10)
  blocking collectives: 1250 us -> 0 us
  waiting for transfers between devices: 796 us -> 0 us
  Pallas kernels: 0 us -> 209 us
  matrix products: 88.5 us -> 0 us
  local copies, waits for them, and re-layouts: 53.7 us -> 6.12 us
    psum x12 -> x0, blocking collectives: 908 us -> none  [on_device(): squares = lax.psum(jnp.sum(image * image, axis=1), ('grp', 'blk'))]
    all_gather x12 -> x0, waiting for transfers between devices: 795 us -> none  [on_device(): piece = lax.all_gather(beside_all, 'grp', axis=1, tiled=True)]
    all_gather x12 -> x0, blocking collectives: 338 us -> none  [on_device(): beside_all = lax.all_gather(basis, 'blk', axis=1, tiled=True)]
    pallas_call x0 -> x1, Pallas kernels: none -> 209 us  [on_device(): pl.pallas_call(kernel, out_shape=(jax.ShapeDtypeStruct((32, KEEP), BF16),...]
    dot_general x14 -> x0, matrix products: 88.5 us -> none  [the longest x12 87.5 us: on_device(): jnp.einsum('rbgc,sgbc->srbg', tile_grid, piece.reshape(scen_count, shard_...]
    reshape x13 -> x0, local copies, waits for them, and re-layouts: 42.9 us -> none  [the longest x12 36.4 us: on_device(): piece.reshape(scen_count, shard_count, cycle_size, tile_rows)]
  transfers between devices with their start and end apart: 12 -> 0, of which waited for: 12 -> 0; matrix products, arithmetic and copies ran while one was open for 0% -> 0% of each run, Pallas kernels for 0% -> 0%
where the time goes in v1:
time: 216 us
  Pallas kernels  209 us (97%)
  local copies, waits for them, and re-layouts  6.12 us (3%)
    pallas_call x1, Pallas kernels, on_device(): pl.pallas_call(kernel, out_shape=(jax.ShapeDtypeStruct((32, KEEP), BF16),...  209 us
    unnamed x14, local copies, waits for them, and re-layouts  6.12 us

profile of v1, /device:TPU:1, one launch (start us, length us, event | category | flops | bytes accessed | tf_op | source)
XLA Modules:
  0.0 215.7 jit_solution(8707508985214739375)
XLA Ops:
  0.6 0.0 copy-start
  0.6 1.6 copy-done
  2.2 0.0 copy-start.1
  2.2 0.7 copy-done.1
  2.9 0.0 copy-start.2
  2.9 0.7 copy-done.2
  3.6 0.0 copy-start.3
  3.6 0.7 copy-done.3
  4.3 0.0 copy-start.4
  4.3 0.7 copy-done.4
  4.9 0.0 copy-start.5
  4.9 0.7 copy-done.5
  5.6 208.9 %krylov.1 = (bf16[32,64]{1,0:T(8,128)(2,1)S(1)}, f32[12,32]{1,0:T(8,128)S(1)}) custom-call(bf16[64,16384]{1,0:T(8,128)(2,1)S(1)} %copy-done, s32[1,256]{1,0:T(1,128)S(1)} %copy-done.2, bf16[32,64]{1,0:T(8,128)(2,1)S(1)} %copy-done.1, s32[1,64]{1,0:T(1,128)S(1)} %bitcast.3, f32[1,64]{1,0:T(1,128)S(1)} %bitcast.4, s32[1,32]{1,0:T(1,128)S(1)} %bitcast.5), custom_call_target="tpu_custom_call" | custom-call | flops 805306368 | bytes 2097152 | tf_op jit(solution)/shard_map/krylov/pallas_call | solution.py:217
  214.5 0.6 copy.10
  215.1 0.6 copy.11
Async XLA Ops:
  0.6 1.6 copy-start
  2.2 0.7 copy-start.1
  2.9 0.7 copy-start.2
  3.6 0.7 copy-start.3
  4.3 0.7 copy-start.4
  4.9 0.7 copy-start.5

commit v2 on v1

--- a/solution.py
+++ b/solution.py
@@ -22,14 +22,30 @@
     return sum(min(d, n - d) for d, n in zip(delta, (NX, NY, NZ)))
 
 
-DELTAS = sorted(
-    [(dx, dy, dz) for dz in range(NZ) for dx in range(NX) for dy in range(NY) if dx or dy or dz],
+ORDER = (0, 1, 7, 2, 6, 3, 5, 4)
+PLACE = {dz: i for i, dz in enumerate(ORDER)}
+GROUPS = ((1, 3), (3, 7))
+PLANE = sorted(
+    [(dx, dy, 0) for dx in range(NX) for dy in range(NY) if dx or dy], key=lambda d: -hops(d)
+)
+LISTED = [p for lo, hi in GROUPS for p in range(lo, hi)]
+ABOVE = [dz for dz in (3, 5, 2, 6, 1, 7, 4) if PLACE[(NZ - dz) % NZ] in LISTED]
+DIRECT = sorted(
+    [
+        (dx, dy, dz)
+        for dz in range(NZ)
+        for dx in range(NX)
+        for dy in range(NY)
+        if (dx or dy or dz) and PLACE[(NZ - dz) % NZ] not in LISTED
+    ],
     key=lambda d: -hops(d),
 )
-
-
-def device(x, y, z, core):
-    return {"blk": lax.div(y, 2) * NX + x, "grp": lax.rem(y, 2) * 16 + z * 2 + core}
+DUE = len(DIRECT) + len(PLANE) * len(LISTED)
+SLOTS = 3
+
+
+def device(blk, grp):
+    return {"blk": blk, "grp": grp}
 
 
 def iota(shape, dim):
@@ -43,28 +59,48 @@
 
 
 def kernel(
-    tiles, expo, rhs, frac, comp, smap, basis_out, rms_out,
-    amat, vbuf, start, started, diag_mine, diag_other, gains, norms, history, last,
-    load_sem, swap_send, swap_recv, send, recv,
+    tiles, expo_in, rhs_in, frac_in, comp_in, smap_in, basis_out, rms_out,
+    expo, rhs, frac, comp, smap, raw, amat, vbuf, start, started, diag_mine, diag_other, gains, norms, history, last,
+    load_sem, swap_send, swap_recv, send, recv, relay, norm_sem,
 ):
     blk, grp = lax.axis_index("blk"), lax.axis_index("grp")
     x, y = lax.rem(blk, NX), lax.div(blk, NX) * 2 + lax.div(grp, 16)
     z, core = lax.rem(lax.div(grp, 2), NZ), lax.rem(grp, 2)
     other = 1 - core
     mine = lax.div(y, 2) * 64 + x * 16 + lax.rem(y, 2) * 8 + z
-    sibling = device(x, y, z, other)
-    peers = [
-        device(lax.rem(x + dx, NX), lax.rem(y + dy, NY), lax.rem(z + dz, NZ), core)
-        for dx, dy, dz in DELTAS
+    sibling = device(blk, grp + 1 - 2 * core)
+    xs = [lax.rem(x + d, NX) for d in range(NX)]
+    ys = [lax.rem(y + d, NY) for d in range(NY)]
+    blks = [[lax.div(ys[dy], 2) * NX + xs[dx] for dy in range(NY)] for dx in range(NX)]
+    low = [lax.rem(y, 2) * 16 + core, (1 - lax.rem(y, 2)) * 16 + core]
+    grps = [[low[d] + 2 * lax.rem(z + dz, NZ) for dz in range(NZ)] for d in range(2)]
+
+    def peer(delta):
+        dx, dy, dz = delta
+        return device(blks[dx][dy], grps[dy % 2][dz])
+
+    everyone = sorted((dx, dy, dz) for dz in range(NZ) for dx in range(NX) for dy in range(NY))[1:]
+    everyone.sort(key=lambda d: -hops(d))
+    base = mine - z
+
+    own_rows = pl.ds(pl.multiple_of(core * KEEP, KEEP), KEEP)
+    load = pltpu.make_async_copy(tiles, raw.at[own_rows], load_sem.at[0])
+    load.start()
+    small = [
+        pltpu.make_async_copy(src, dst, load_sem.at[1 + i])
+        for i, (src, dst) in enumerate(
+            [(expo_in, expo), (rhs_in, rhs), (frac_in, frac), (comp_in, comp), (smap_in, smap)]
+        )
     ]
-
-    own_rows = pl.ds(pl.multiple_of(core * KEEP, KEEP), KEEP)
-    load = pltpu.make_async_copy(tiles, amat.at[own_rows], load_sem)
-    load.start()
+    for copy in small:
+        copy.start()
 
     barrier = pltpu.get_barrier_semaphore()
-    for peer in [sibling, *peers]:
-        pl.semaphore_signal(barrier, inc=1, device_id=peer, device_id_type=MESH)
+    for to in [sibling, *(peer(d) for d in everyone)]:
+        pl.semaphore_signal(barrier, inc=1, device_id=to, device_id_type=MESH)
+
+    for copy in small:
+        copy.wait()
 
     picked = as_column(smap[...].astype(F32)) == iota((32, 32), 1).astype(F32)
     first = jnp.dot(
@@ -89,35 +125,6 @@
     ).astype(BF16)
     gains[...] = jnp.dot(spread, sides, preferred_element_type=F32)
 
-    pl.semaphore_wait(barrier, 1 + len(peers))
-
-    def swap(src, dst, i):
-        return pltpu.make_async_remote_copy(
-            src, dst, swap_send.at[i], swap_recv.at[i], device_id=sibling, device_id_type=MESH
-        )
-
-    swap_start = swap(start.at[other], started, 0)
-    swap_start.start()
-    swap_diag = swap(diag_mine, diag_other, 1)
-    swap_diag.start()
-
-    ours = (iota((1, ROWS), 1) >> 6) == core
-
-    def whole(sem, par):
-        part = vbuf.at[par, pl.ds(0, CHIPS - 1)]
-        return pltpu.make_async_copy(part, part, sem.at[par])
-
-    def post(par):
-        block = vbuf.at[par, mine]
-        for peer in peers:
-            pltpu.make_async_remote_copy(
-                block, block, send.at[par], recv.at[par], device_id=peer, device_id_type=MESH
-            ).start()
-
-    swap_start.wait()
-    vbuf[0, mine] = jnp.where(ours, start[core], started[...])
-    post(0)
-
     load.wait()
 
     def scale(b, _):
@@ -125,20 +132,82 @@
         columns = pl.ds(pl.multiple_of(b * ROWS, ROWS), ROWS)
         for i in range(KEEP // 16):
             rows = pl.ds(pl.multiple_of(core * KEEP + 16 * i, 16), 16)
-            amat[rows, columns] = amat[rows, columns] * gain
+            raw[rows, columns] = raw[rows, columns] * gain
         return 0
 
     lax.fori_loop(0, CHIPS, scale, 0, unroll=4)
-    swap_rows = swap(amat.at[own_rows], amat.at[own_rows], 2)
+
+    pl.semaphore_wait(barrier, CHIPS)
+
+    def swap(src, dst, i):
+        return pltpu.make_async_remote_copy(
+            src, dst, swap_send.at[i], swap_recv.at[i], device_id=sibling, device_id_type=MESH
+        )
+
+    swap_start = swap(start.at[other], started, 0)
+    swap_start.start()
+    swap_diag = swap(diag_mine, diag_other, 1)
+    swap_diag.start()
+
+    ours = (iota((1, ROWS), 1) >> 6) == core
+
+    def blocks(sem, slot, count):
+        part = vbuf.at[slot, pl.ds(0, count)]
+        return pltpu.make_async_copy(part, part, sem)
+
+    def send_to(slot, at, there, count, delta, sem):
+        pltpu.make_async_remote_copy(
+            vbuf.at[slot, pl.ds(at, count)], vbuf.at[slot, pl.ds(there, count)],
+            send.at[slot], sem, device_id=peer(delta), device_id_type=MESH,
+        ).start()
+
+    def post(slot):
+        for dz in ABOVE:
+            place = PLACE[NZ - dz]
+            group = [lo <= place < hi for lo, hi in GROUPS].index(True)
+            send_to(slot, base, base + place, 1, (0, 0, dz), relay.at[slot, group])
+        for delta in DIRECT:
+            place = PLACE[(NZ - delta[2]) % NZ]
+            send_to(slot, base, base + place, 1, delta, recv.at[slot])
+
+    def pass_on(slot):
+        for i, (lo, hi) in enumerate(GROUPS):
+            blocks(relay.at[slot, i], slot, hi - max(lo, 1)).wait()
+            for delta in PLANE:
+                send_to(slot, base + lo, base + lo, hi - lo, delta, recv.at[slot])
+
+    def sent(slot):
+        return blocks(send.at[slot], slot, len(ABOVE) + DUE)
+
+    swap_start.wait()
+    vbuf[0, base] = jnp.where(ours, start[core], started[...])
+    post(0)
+
+    swap_rows = swap(raw.at[own_rows], raw.at[own_rows], 2)
     swap_rows.start()
+    pass_on(0)
     swap_diag.wait()
     diag = jnp.where(ours, diag_mine[0:1], diag_other[0:1])
     swap_rows.wait()
 
+    eye_rows = jnp.where(iota((ROWS, ROWS), 0) == iota((ROWS, ROWS), 1), 1.0, 0.0).astype(BF16)
+
+    def turn(column, _):
+        for place, dz in enumerate(ORDER):
+            source = column * NZ + lax.rem(z + dz, NZ)
+            rows = pl.ds(pl.multiple_of((column * NZ + place) * ROWS, ROWS), ROWS)
+            amat[rows, :] = lax.dot_general(
+                eye_rows, raw[:, pl.ds(pl.multiple_of(source * ROWS, ROWS), ROWS)],
+                (((1,), (1,)), ((), ())), preferred_element_type=F32,
+            ).astype(BF16)
+        return 0
+
+    lax.fori_loop(0, NX * NY, turn, 0)
+
     lane = iota((HALF, ROWS), 1)
 
     def product(step, par):
-        whole(recv, par).wait()
+        blocks(recv.at[par], par, DUE).wait()
         sums = [jnp.zeros((HALF, ROWS), F32) for _ in range(4)]
         for b in range(CHIPS):
             value = vbuf[par, b].astype(F32)
@@ -158,40 +227,40 @@
                 [vbuf[par, g * group + i] * spread16 for i in range(group)], axis=1
             )
             total += lax.dot_general(
-                part, amat[:, g * group * ROWS : (g + 1) * group * ROWS],
-                (((1,), (1,)), ((), ())), preferred_element_type=F32,
+                part, amat[g * group * ROWS : (g + 1) * group * ROWS, :],
+                (((1,), (0,)), ((), ())), preferred_element_type=F32,
             )
-        own = vbuf[par, mine].astype(F32)
+        own = vbuf[par, base].astype(F32)
         return total * (inverse / shrink) + diag * (own * inverse)
 
     history[core] = jnp.zeros((HALF, ROWS), F32)
 
     def advance(step, _):
-        par = lax.rem(step, 2)
+        par, nxt = lax.rem(step, SLOTS), lax.rem(step + 1, SLOTS)
         image = product(step, par)
 
         @pl.when(step >= 1)
         def _():
-            whole(send, 1 - par).wait()
-
-        vbuf[1 - par, mine] = image.astype(BF16)
-        post(1 - par)
+            sent(lax.rem(step + SLOTS - 1, SLOTS)).wait()
+
+        vbuf[nxt, base] = image.astype(BF16)
+        post(nxt)
+        pass_on(nxt)
         return 0
 
     lax.fori_loop(0, STEPS - 1, advance, 0)
-    image = product(STEPS - 1, (STEPS - 1) % 2)
+    image = product(STEPS - 1, (STEPS - 1) % SLOTS)
 
     eye = iota((HALF, ROWS), 0) == lane
     square = jnp.sum(image * image, axis=1, keepdims=True)
     norms[pl.ds(mine, 1), :] = jnp.sum(jnp.where(eye, square, 0.0), axis=0, keepdims=True)
-    whole(send, 0).wait()
     row = norms.at[pl.ds(mine, 1)]
-    for peer in peers:
+    for delta in everyone:
         pltpu.make_async_remote_copy(
-            row, row, send.at[0], recv.at[0], device_id=peer, device_id_type=MESH
+            row, row, norm_sem.at[0], norm_sem.at[1], device_id=peer(delta), device_id_type=MESH
         ).start()
     rows = norms.at[pl.ds(0, CHIPS - 1)]
-    pltpu.make_async_copy(rows, rows, recv.at[0]).wait()
+    pltpu.make_async_copy(rows, rows, norm_sem.at[1]).wait()
     total = jnp.sum(norms[...], axis=0, keepdims=True)
     squares = jnp.sum(jnp.where(eye, total, 0.0), axis=1, keepdims=True)
     root = jnp.sqrt(squares / ALL + 1e-06)
@@ -201,8 +270,9 @@
     swap_history = swap(history.at[core], history.at[core], 4)
     swap_last.start()
     swap_history.start()
-    pltpu.make_async_copy(rows, rows, send.at[0]).wait()
-    whole(send, 1).wait()
+    pltpu.make_async_copy(rows, rows, norm_sem.at[0]).wait()
+    sent((STEPS - 2) % SLOTS).wait()
+    sent((STEPS - 1) % SLOTS).wait()
     swap_last.wait()
     swap_history.wait()
     result = jnp.concatenate([last[0], last[1]], axis=0).astype(F32)
@@ -220,11 +290,17 @@
                 jax.ShapeDtypeStruct((32, KEEP), BF16),
                 jax.ShapeDtypeStruct((STEPS, 32), F32),
             ),
-            in_specs=[pl.BlockSpec(memory_space=pl.ANY)] + [vmem] * 5,
+            in_specs=[pl.BlockSpec(memory_space=pltpu.HBM)] * 6,
             out_specs=(vmem, vmem),
             scratch_shapes=[
+                pltpu.VMEM((1, 256), jnp.int32),
+                pltpu.VMEM((32, KEEP), BF16),
+                pltpu.VMEM((1, KEEP), jnp.int32),
+                pltpu.VMEM((1, 64), F32),
+                pltpu.VMEM((1, 32), jnp.int32),
                 pltpu.VMEM((ROWS, ALL), BF16),
-                pltpu.VMEM((2, CHIPS, HALF, ROWS), BF16),
+                pltpu.VMEM((ALL, ROWS), BF16),
+                pltpu.VMEM((SLOTS, CHIPS, HALF, ROWS), BF16),
                 pltpu.VMEM((2, HALF, ROWS), BF16),
                 pltpu.VMEM((HALF, ROWS), BF16),
                 pltpu.VMEM((8, ROWS), F32),
@@ -233,14 +309,16 @@
                 pltpu.VMEM((CHIPS, ROWS), F32),
                 pltpu.VMEM((2, HALF, ROWS), F32),
                 pltpu.VMEM((2, HALF, ROWS), BF16),
-                pltpu.SemaphoreType.DMA,
+                pltpu.SemaphoreType.DMA((6,)),
                 pltpu.SemaphoreType.DMA((5,)),
                 pltpu.SemaphoreType.DMA((5,)),
-                pltpu.SemaphoreType.DMA((2,)),
+                pltpu.SemaphoreType.DMA((SLOTS,)),
+                pltpu.SemaphoreType.DMA((SLOTS,)),
+                pltpu.SemaphoreType.DMA((SLOTS, NZ - 1)),
                 pltpu.SemaphoreType.DMA((2,)),
             ],
             compiler_params=pltpu.CompilerParams(
-                collective_id=0, has_side_effects=True, vmem_limit_bytes=32 << 20
+                collective_id=0, has_side_effects=True, vmem_limit_bytes=63 << 20
             ),
             cost_estimate=pl.CostEstimate(
                 flops=2 * STEPS * 32 * KEEP * ALL, bytes_accessed=2 * KEEP * ALL, transcendentals=0

time: 216 us -> 163 us (0.75)
  Pallas kernels: 209 us -> 159 us
  local copies, waits for them, and re-layouts: 6.12 us -> 2.59 us
    pallas_call x1, Pallas kernels: 209 us -> 159 us  [on_device(): pl.pallas_call(kernel, out_shape=(jax.ShapeDtypeStruct((32, KEEP), BF16),...]
    unnamed x14 -> x2, local copies, waits for them, and re-layouts: 6.12 us -> 2.59 us
where the time goes in v2:
time: 163 us
  Pallas kernels  159 us (98%)
  local copies, waits for them, and re-layouts  2.59 us (2%)
    pallas_call x1, Pallas kernels, on_device(): pl.pallas_call(kernel, out_shape=(jax.ShapeDtypeStruct((32, KEEP), BF16),...  159 us

profile of v2, /device:TPU:1, one launch (start us, length us, event | category | flops | bytes accessed | tf_op | source)
XLA Modules:
  0.0 162.6 jit_solution(2771460678293744650)
XLA Ops:
  0.6 159.4 %krylov.1 = (bf16[32,64]{1,0:T(8,128)(2,1)}, f32[12,32]{1,0:T(8,128)}) custom-call(bf16[64,16384]{1,0:T(8,128)(2,1)} %tiles.1, s32[1,256]{1,0:T(1,128)} %expo_in.1, bf16[32,64]{1,0:T(8,128)(2,1)} %rhs_in.1, s32[1,64]{1,0:T(1,128)} %bitcast.3, f32[1,64]{1,0:T(1,128)} %bitcast.4, s32[1,32]{1,0:T(1,128)} %bitcast.5), custom_call_target="tpu_custom_call" | custom-call | flops 805306368 | bytes 2097152 | tf_op jit(solution)/shard_map/krylov/pallas_call | solution.py:287
  160.0 1.3 copy.10
  161.3 1.3 copy.11

commit v3 on v2

--- a/solution.py
+++ b/solution.py
@@ -24,23 +24,28 @@
 
 ORDER = (0, 1, 7, 2, 6, 3, 5, 4)
 PLACE = {dz: i for i, dz in enumerate(ORDER)}
-GROUPS = ((1, 3), (3, 7))
+GROUPS = ((1, 2), (2, 3), (3, 7), (7, 8))
+FAR = 6
 PLANE = sorted(
     [(dx, dy, 0) for dx in range(NX) for dy in range(NY) if dx or dy], key=lambda d: -hops(d)
 )
-LISTED = [p for lo, hi in GROUPS for p in range(lo, hi)]
-ABOVE = [dz for dz in (3, 5, 2, 6, 1, 7, 4) if PLACE[(NZ - dz) % NZ] in LISTED]
-DIRECT = sorted(
-    [
-        (dx, dy, dz)
-        for dz in range(NZ)
-        for dx in range(NX)
-        for dy in range(NY)
-        if (dx or dy or dz) and PLACE[(NZ - dz) % NZ] not in LISTED
-    ],
-    key=lambda d: -hops(d),
-)
-DUE = len(DIRECT) + len(PLANE) * len(LISTED)
+ABOVE = [(0, 0, dz) for dz in (4, 3, 5, 2, 6, 1, 7)]
+DUE = CHIPS - NZ
+
+
+def direct(far):
+    return sorted(
+        [
+            (dx, dy, dz)
+            for dz in range(NZ)
+            for dx, dy, _ in PLANE
+            if not dz or hops((dx, dy, dz)) >= far
+        ],
+        key=lambda d: -hops(d),
+    )
+
+
+NEVER = 9
 SLOTS = 3
 
 
@@ -60,14 +65,13 @@
 
 def kernel(
     tiles, expo_in, rhs_in, frac_in, comp_in, smap_in, basis_out, rms_out,
-    expo, rhs, frac, comp, smap, raw, amat, vbuf, start, started, diag_mine, diag_other, gains, norms, history, last,
-    load_sem, swap_send, swap_recv, send, recv, relay, norm_sem,
+    expo, rhs, frac, comp, smap, raw, amat, vbuf, start, started, diag_mine, diag_other, gains, norms, plane, history, last,
+    load_sem, swap_send, swap_recv, send, recv, relay, norm_send, norm_recv,
 ):
     blk, grp = lax.axis_index("blk"), lax.axis_index("grp")
     x, y = lax.rem(blk, NX), lax.div(blk, NX) * 2 + lax.div(grp, 16)
     z, core = lax.rem(lax.div(grp, 2), NZ), lax.rem(grp, 2)
     other = 1 - core
-    mine = lax.div(y, 2) * 64 + x * 16 + lax.rem(y, 2) * 8 + z
     sibling = device(blk, grp + 1 - 2 * core)
     xs = [lax.rem(x + d, NX) for d in range(NX)]
     ys = [lax.rem(y + d, NY) for d in range(NY)]
@@ -79,9 +83,9 @@
         dx, dy, dz = delta
         return device(blks[dx][dy], grps[dy % 2][dz])
 
-    everyone = sorted((dx, dy, dz) for dz in range(NZ) for dx in range(NX) for dy in range(NY))[1:]
-    everyone.sort(key=lambda d: -hops(d))
-    base = mine - z
+    known = ABOVE + PLANE
+    column = lax.div(y, 2) * 8 + x * 2 + lax.rem(y, 2)
+    base = column * NZ
 
     own_rows = pl.ds(pl.multiple_of(core * KEEP, KEEP), KEEP)
     load = pltpu.make_async_copy(tiles, raw.at[own_rows], load_sem.at[0])
@@ -96,7 +100,7 @@
         copy.start()
 
     barrier = pltpu.get_barrier_semaphore()
-    for to in [sibling, *(peer(d) for d in everyone)]:
+    for to in [sibling, *(peer(d) for d in known)]:
         pl.semaphore_signal(barrier, inc=1, device_id=to, device_id_type=MESH)
 
     for copy in small:
@@ -109,6 +113,15 @@
     first = jnp.concatenate([first, first], axis=1).astype(BF16)
     start[0] = first[:HALF]
     start[1] = first[HALF:]
+    pl.semaphore_wait(barrier, 1 + len(known))
+
+    def swap(src, dst, i):
+        return pltpu.make_async_remote_copy(
+            src, dst, swap_send.at[i], swap_recv.at[i], device_id=sibling, device_id_type=MESH
+        )
+
+    swap_start = swap(start.at[other], started, 0)
+    swap_start.start()
     member = iota((64, KEEP), 0) == frac[...]
     local_diag = jnp.sum(
         jnp.where(member, as_column(comp[...]), 0.0), axis=0, keepdims=True
@@ -116,6 +129,45 @@
     diag_mine[...] = jnp.broadcast_to(
         jnp.concatenate([local_diag, local_diag], axis=1), (8, ROWS)
     )
+    swap_diag = swap(diag_mine, diag_other, 1)
+    swap_diag.start()
+
+    ours = (iota((1, ROWS), 1) >> 6) == core
+
+    def blocks(sem, slot, count):
+        part = vbuf.at[slot, pl.ds(0, count)]
+        return pltpu.make_async_copy(part, part, sem)
+
+    def send_to(slot, at, there, count, delta, sem):
+        pltpu.make_async_remote_copy(
+            vbuf.at[slot, pl.ds(at, count)], vbuf.at[slot, pl.ds(there, count)],
+            send.at[slot], sem, device_id=peer(delta), device_id_type=MESH,
+        ).start()
+
+    def post(slot, far=FAR):
+        for delta in ABOVE:
+            place = PLACE[NZ - delta[2]]
+            group = [lo <= place < hi for lo, hi in GROUPS].index(True)
+            send_to(slot, base, base + place, 1, delta, relay.at[slot, group])
+        for delta in direct(far):
+            place = PLACE[(NZ - delta[2]) % NZ]
+            send_to(slot, base, base + place, 1, delta, recv.at[slot])
+
+    def pass_on(slot, far=FAR):
+        for i, (lo, hi) in enumerate(GROUPS):
+            blocks(relay.at[slot, i], slot, hi - lo).wait()
+            for delta in PLANE:
+                count = sum(hops((*delta[:2], ORDER[p])) < far for p in range(lo, hi))
+                if count:
+                    send_to(slot, base + lo, base + lo, count, delta, recv.at[slot])
+
+    def sent(slot):
+        return blocks(send.at[slot], slot, CHIPS - 1)
+
+    swap_start.wait()
+    vbuf[0, base] = jnp.where(ours, start[core], started[...])
+    post(0, NEVER)
+
     scale_row = jnp.exp2(expo[...].astype(F32)).astype(BF16).astype(F32)
     spread = jnp.where(
         (iota((CHIPS, 256), 1) >> 1) == iota((CHIPS, 256), 0), scale_row, 0.0
@@ -137,72 +189,12 @@
 
     lax.fori_loop(0, CHIPS, scale, 0, unroll=4)
 
-    pl.semaphore_wait(barrier, CHIPS)
-
-    def swap(src, dst, i):
-        return pltpu.make_async_remote_copy(
-            src, dst, swap_send.at[i], swap_recv.at[i], device_id=sibling, device_id_type=MESH
-        )
-
-    swap_start = swap(start.at[other], started, 0)
-    swap_start.start()
-    swap_diag = swap(diag_mine, diag_other, 1)
-    swap_diag.start()
-
-    ours = (iota((1, ROWS), 1) >> 6) == core
-
-    def blocks(sem, slot, count):
-        part = vbuf.at[slot, pl.ds(0, count)]
-        return pltpu.make_async_copy(part, part, sem)
-
-    def send_to(slot, at, there, count, delta, sem):
-        pltpu.make_async_remote_copy(
-            vbuf.at[slot, pl.ds(at, count)], vbuf.at[slot, pl.ds(there, count)],
-            send.at[slot], sem, device_id=peer(delta), device_id_type=MESH,
-        ).start()
-
-    def post(slot):
-        for dz in ABOVE:
-            place = PLACE[NZ - dz]
-            group = [lo <= place < hi for lo, hi in GROUPS].index(True)
-            send_to(slot, base, base + place, 1, (0, 0, dz), relay.at[slot, group])
-        for delta in DIRECT:
-            place = PLACE[(NZ - delta[2]) % NZ]
-            send_to(slot, base, base + place, 1, delta, recv.at[slot])
-
-    def pass_on(slot):
-        for i, (lo, hi) in enumerate(GROUPS):
-            blocks(relay.at[slot, i], slot, hi - max(lo, 1)).wait()
-            for delta in PLANE:
-                send_to(slot, base + lo, base + lo, hi - lo, delta, recv.at[slot])
-
-    def sent(slot):
-        return blocks(send.at[slot], slot, len(ABOVE) + DUE)
-
-    swap_start.wait()
-    vbuf[0, base] = jnp.where(ours, start[core], started[...])
-    post(0)
-
     swap_rows = swap(raw.at[own_rows], raw.at[own_rows], 2)
     swap_rows.start()
-    pass_on(0)
+    pass_on(0, NEVER)
     swap_diag.wait()
     diag = jnp.where(ours, diag_mine[0:1], diag_other[0:1])
     swap_rows.wait()
-
-    eye_rows = jnp.where(iota((ROWS, ROWS), 0) == iota((ROWS, ROWS), 1), 1.0, 0.0).astype(BF16)
-
-    def turn(column, _):
-        for place, dz in enumerate(ORDER):
-            source = column * NZ + lax.rem(z + dz, NZ)
-            rows = pl.ds(pl.multiple_of((column * NZ + place) * ROWS, ROWS), ROWS)
-            amat[rows, :] = lax.dot_general(
-                eye_rows, raw[:, pl.ds(pl.multiple_of(source * ROWS, ROWS), ROWS)],
-                (((1,), (1,)), ((), ())), preferred_element_type=F32,
-            ).astype(BF16)
-        return 0
-
-    lax.fori_loop(0, NX * NY, turn, 0)
 
     lane = iota((HALF, ROWS), 1)
 
@@ -214,9 +206,7 @@
             sums[b % 4] += value * value
         squares = jnp.sum((sums[0] + sums[1]) + (sums[2] + sums[3]), axis=1, keepdims=True)
         root = jnp.sqrt(squares / ALL + 1e-06)
-        opening = step == 0
         history[core] = jnp.where(lane == step - 1, root, history[core])
-        root = jnp.where(opening, 1.0, root)
         shrink = jnp.exp2(-jnp.floor(jnp.log2(root))).astype(BF16).astype(F32)
         inverse = 1.0 / root
         spread16 = jnp.broadcast_to(shrink, (HALF, ROWS)).astype(BF16)
@@ -235,33 +225,71 @@
 
     history[core] = jnp.zeros((HALF, ROWS), F32)
 
+    blocks(recv.at[0], 0, DUE).wait()
+
+    def column_product(column, total):
+        parts, rows = [], []
+        for place, dz in enumerate(ORDER):
+            source = column * NZ + lax.rem(z + dz, NZ)
+            parts.append(vbuf[0, column * NZ + place])
+            rows.append(raw[:, pl.ds(pl.multiple_of(source * ROWS, ROWS), ROWS)])
+        return total + lax.dot_general(
+            jnp.concatenate(parts, axis=1), jnp.concatenate(rows, axis=1),
+            (((1,), (1,)), ((), ())), preferred_element_type=F32,
+        )
+
+    total = lax.fori_loop(
+        0, NX * NY, column_product, jnp.zeros((HALF, ROWS), F32), unroll=4
+    )
+    image = total + diag * vbuf[0, base].astype(F32)
+    vbuf[1, base] = image.astype(BF16)
+    post(1)
+    pass_on(1)
+
+    eye_rows = jnp.where(iota((ROWS, ROWS), 0) == iota((ROWS, ROWS), 1), 1.0, 0.0).astype(BF16)
+
+    def turn(column, _):
+        for place, dz in enumerate(ORDER):
+            source = column * NZ + lax.rem(z + dz, NZ)
+            rows = pl.ds(pl.multiple_of((column * NZ + place) * ROWS, ROWS), ROWS)
+            amat[rows, :] = lax.dot_general(
+                eye_rows, raw[:, pl.ds(pl.multiple_of(source * ROWS, ROWS), ROWS)],
+                (((1,), (1,)), ((), ())), preferred_element_type=F32,
+            ).astype(BF16)
+        return 0
+
+    lax.fori_loop(0, NX * NY, turn, 0)
+
     def advance(step, _):
         par, nxt = lax.rem(step, SLOTS), lax.rem(step + 1, SLOTS)
         image = product(step, par)
-
-        @pl.when(step >= 1)
-        def _():
-            sent(lax.rem(step + SLOTS - 1, SLOTS)).wait()
+        sent(lax.rem(step + SLOTS - 1, SLOTS)).wait()
 
         vbuf[nxt, base] = image.astype(BF16)
         post(nxt)
         pass_on(nxt)
         return 0
 
-    lax.fori_loop(0, STEPS - 1, advance, 0)
+    lax.fori_loop(1, STEPS - 1, advance, 0)
     image = product(STEPS - 1, (STEPS - 1) % SLOTS)
+
+    def sums_of(ref, at, deltas, i):
+        row = ref.at[pl.ds(at, 1)]
+        for delta in deltas:
+            pltpu.make_async_remote_copy(
+                row, row, norm_send.at[i], norm_recv.at[i],
+                device_id=peer(delta), device_id_type=MESH,
+            ).start()
+        rows = ref.at[pl.ds(0, len(deltas))]
+        pltpu.make_async_copy(rows, rows, norm_recv.at[i]).wait()
 
     eye = iota((HALF, ROWS), 0) == lane
     square = jnp.sum(image * image, axis=1, keepdims=True)
-    norms[pl.ds(mine, 1), :] = jnp.sum(jnp.where(eye, square, 0.0), axis=0, keepdims=True)
-    row = norms.at[pl.ds(mine, 1)]
-    for delta in everyone:
-        pltpu.make_async_remote_copy(
-            row, row, norm_sem.at[0], norm_sem.at[1], device_id=peer(delta), device_id_type=MESH
-        ).start()
-    rows = norms.at[pl.ds(0, CHIPS - 1)]
-    pltpu.make_async_copy(rows, rows, norm_sem.at[1]).wait()
-    total = jnp.sum(norms[...], axis=0, keepdims=True)
+    norms[pl.ds(z, 1), :] = jnp.sum(jnp.where(eye, square, 0.0), axis=0, keepdims=True)
+    sums_of(norms, z, ABOVE, 0)
+    plane[pl.ds(column, 1), :] = jnp.sum(norms[...], axis=0, keepdims=True)
+    sums_of(plane, column, PLANE, 1)
+    total = jnp.sum(plane[...], axis=0, keepdims=True)
     squares = jnp.sum(jnp.where(eye, total, 0.0), axis=1, keepdims=True)
     root = jnp.sqrt(squares / ALL + 1e-06)
     history[core] = jnp.where(lane == STEPS - 1, root, history[core])
@@ -270,7 +298,9 @@
     swap_history = swap(history.at[core], history.at[core], 4)
     swap_last.start()
     swap_history.start()
-    pltpu.make_async_copy(rows, rows, norm_sem.at[0]).wait()
+    for ref, i in ((norms, 0), (plane, 1)):
+        rows = ref.at[pl.ds(0, ref.shape[0] - 1)]
+        pltpu.make_async_copy(rows, rows, norm_send.at[i]).wait()
     sent((STEPS - 2) % SLOTS).wait()
     sent((STEPS - 1) % SLOTS).wait()
     swap_last.wait()
@@ -306,7 +336,8 @@
                 pltpu.VMEM((8, ROWS), F32),
                 pltpu.VMEM((8, ROWS), F32),
                 pltpu.VMEM((CHIPS, ROWS), F32),
-                pltpu.VMEM((CHIPS, ROWS), F32),
+                pltpu.VMEM((NZ, ROWS), F32),
+                pltpu.VMEM((NX * NY, ROWS), F32),
                 pltpu.VMEM((2, HALF, ROWS), F32),
                 pltpu.VMEM((2, HALF, ROWS), BF16),
                 pltpu.SemaphoreType.DMA((6,)),
@@ -315,6 +346,7 @@
                 pltpu.SemaphoreType.DMA((SLOTS,)),
                 pltpu.SemaphoreType.DMA((SLOTS,)),
                 pltpu.SemaphoreType.DMA((SLOTS, NZ - 1)),
+                pltpu.SemaphoreType.DMA((2,)),
                 pltpu.SemaphoreType.DMA((2,)),
             ],
             compiler_params=pltpu.CompilerParams(

time: 163 us -> 155 us (0.951)
  Pallas kernels: 159 us -> 152 us
    pallas_call x1, Pallas kernels: 159 us -> 152 us  [on_device(): pl.pallas_call(kernel, out_shape=(jax.ShapeDtypeStruct((32, KEEP), BF16),...]
where the time goes in v3:
time: 155 us
  Pallas kernels  152 us (98%)
  local copies, waits for them, and re-layouts  2.59 us (2%)
    pallas_call x1, Pallas kernels, on_device(): pl.pallas_call(kernel, out_shape=(jax.ShapeDtypeStruct((32, KEEP), BF16),...  152 us

profile of v3, /device:TPU:1, one launch (start us, length us, event | category | flops | bytes accessed | tf_op | source)
XLA Modules:
  0.0 154.9 jit_solution(6919633909741458994)
XLA Ops:
  0.6 151.6 %krylov.1 = (bf16[32,64]{1,0:T(8,128)(2,1)}, f32[12,32]{1,0:T(8,128)}) custom-call(bf16[64,16384]{1,0:T(8,128)(2,1)} %tiles.1, s32[1,256]{1,0:T(1,128)} %expo_in.1, bf16[32,64]{1,0:T(8,128)(2,1)} %rhs_in.1, s32[1,64]{1,0:T(1,128)} %bitcast.3, f32[1,64]{1,0:T(1,128)} %bitcast.4, s32[1,32]{1,0:T(1,128)} %bitcast.5), custom_call_target="tpu_custom_call" | custom-call | flops 805306368 | bytes 2097152 | tf_op jit(solution)/shard_map/krylov/pallas_call | solution.py:317
  152.3 1.3 copy.10
  153.6 1.3 copy.11

commit v4 on v3

--- a/solution.py
+++ b/solution.py
@@ -24,12 +24,16 @@
 
 ORDER = (0, 1, 7, 2, 6, 3, 5, 4)
 PLACE = {dz: i for i, dz in enumerate(ORDER)}
-GROUPS = ((1, 2), (2, 3), (3, 7), (7, 8))
+GROUPS = ((1, 2), (2, 3), (3, 5), (5, 7), (7, 8))
 FAR = 6
 PLANE = sorted(
     [(dx, dy, 0) for dx in range(NX) for dy in range(NY) if dx or dy], key=lambda d: -hops(d)
 )
 ABOVE = [(0, 0, dz) for dz in (4, 3, 5, 2, 6, 1, 7)]
+EVERYONE = sorted(
+    [(dx, dy, dz) for dz in range(NZ) for dx in range(NX) for dy in range(NY) if dx or dy or dz],
+    key=lambda d: -hops(d),
+)
 DUE = CHIPS - NZ
 
 
@@ -41,7 +45,7 @@
             for dx, dy, _ in PLANE
             if not dz or hops((dx, dy, dz)) >= far
         ],
-        key=lambda d: -hops(d),
+        key=lambda d: (-hops(d), -min(d[2], NZ - d[2]), d),
     )
 
 
@@ -65,7 +69,7 @@
 
 def kernel(
     tiles, expo_in, rhs_in, frac_in, comp_in, smap_in, basis_out, rms_out,
-    expo, rhs, frac, comp, smap, raw, amat, vbuf, start, started, diag_mine, diag_other, gains, norms, plane, history, last,
+    expo, rhs, frac, comp, smap, raw, amat, vbuf, start, started, diag_mine, diag_other, gains, norms, history, last,
     load_sem, swap_send, swap_recv, send, recv, relay, norm_send, norm_recv,
 ):
     blk, grp = lax.axis_index("blk"), lax.axis_index("grp")
@@ -273,23 +277,17 @@
     lax.fori_loop(1, STEPS - 1, advance, 0)
     image = product(STEPS - 1, (STEPS - 1) % SLOTS)
 
-    def sums_of(ref, at, deltas, i):
-        row = ref.at[pl.ds(at, 1)]
-        for delta in deltas:
-            pltpu.make_async_remote_copy(
-                row, row, norm_send.at[i], norm_recv.at[i],
-                device_id=peer(delta), device_id_type=MESH,
-            ).start()
-        rows = ref.at[pl.ds(0, len(deltas))]
-        pltpu.make_async_copy(rows, rows, norm_recv.at[i]).wait()
-
     eye = iota((HALF, ROWS), 0) == lane
     square = jnp.sum(image * image, axis=1, keepdims=True)
-    norms[pl.ds(z, 1), :] = jnp.sum(jnp.where(eye, square, 0.0), axis=0, keepdims=True)
-    sums_of(norms, z, ABOVE, 0)
-    plane[pl.ds(column, 1), :] = jnp.sum(norms[...], axis=0, keepdims=True)
-    sums_of(plane, column, PLANE, 1)
-    total = jnp.sum(plane[...], axis=0, keepdims=True)
+    norms[pl.ds(base + z, 1), :] = jnp.sum(jnp.where(eye, square, 0.0), axis=0, keepdims=True)
+    row = norms.at[pl.ds(base + z, 1)]
+    for delta in EVERYONE:
+        pltpu.make_async_remote_copy(
+            row, row, norm_send, norm_recv, device_id=peer(delta), device_id_type=MESH
+        ).start()
+    rows = norms.at[pl.ds(0, CHIPS - 1)]
+    pltpu.make_async_copy(rows, rows, norm_recv).wait()
+    total = jnp.sum(norms[...], axis=0, keepdims=True)
     squares = jnp.sum(jnp.where(eye, total, 0.0), axis=1, keepdims=True)
     root = jnp.sqrt(squares / ALL + 1e-06)
     history[core] = jnp.where(lane == STEPS - 1, root, history[core])
@@ -298,9 +296,7 @@
     swap_history = swap(history.at[core], history.at[core], 4)
     swap_last.start()
     swap_history.start()
-    for ref, i in ((norms, 0), (plane, 1)):
-        rows = ref.at[pl.ds(0, ref.shape[0] - 1)]
-        pltpu.make_async_copy(rows, rows, norm_send.at[i]).wait()
+    pltpu.make_async_copy(rows, rows, norm_send).wait()
     sent((STEPS - 2) % SLOTS).wait()
     sent((STEPS - 1) % SLOTS).wait()
     swap_last.wait()
@@ -336,8 +332,7 @@
                 pltpu.VMEM((8, ROWS), F32),
                 pltpu.VMEM((8, ROWS), F32),
                 pltpu.VMEM((CHIPS, ROWS), F32),
-                pltpu.VMEM((NZ, ROWS), F32),
-                pltpu.VMEM((NX * NY, ROWS), F32),
+                pltpu.VMEM((CHIPS, ROWS), F32),
                 pltpu.VMEM((2, HALF, ROWS), F32),
                 pltpu.VMEM((2, HALF, ROWS), BF16),
                 pltpu.SemaphoreType.DMA((6,)),
@@ -346,8 +341,8 @@
                 pltpu.SemaphoreType.DMA((SLOTS,)),
                 pltpu.SemaphoreType.DMA((SLOTS,)),
                 pltpu.SemaphoreType.DMA((SLOTS, NZ - 1)),
-                pltpu.SemaphoreType.DMA((2,)),
-                pltpu.SemaphoreType.DMA((2,)),
+                pltpu.SemaphoreType.DMA,
+                pltpu.SemaphoreType.DMA,
             ],
             compiler_params=pltpu.CompilerParams(
                 collective_id=0, has_side_effects=True, vmem_limit_bytes=63 << 20

time: 155 us -> 153 us (0.987)
  Pallas kernels: 152 us -> 150 us
    pallas_call x1, Pallas kernels: 152 us -> 150 us  [on_device(): pl.pallas_call(kernel, out_shape=(jax.ShapeDtypeStruct((32, KEEP), BF16),...]
where the time goes in v4:
time: 153 us
  Pallas kernels  150 us (98%)
  local copies, waits for them, and re-layouts  2.59 us (2%)
    pallas_call x1, Pallas kernels, on_device(): pl.pallas_call(kernel, out_shape=(jax.ShapeDtypeStruct((32, KEEP), BF16),...  150 us

profile of v4, /device:TPU:1, one launch (start us, length us, event | category | flops | bytes accessed | tf_op | source)
XLA Modules:
  0.0 153.2 jit_solution(8351948909748571302)
XLA Ops:
  0.6 150.0 %krylov.1 = (bf16[32,64]{1,0:T(8,128)(2,1)}, f32[12,32]{1,0:T(8,128)}) custom-call(bf16[64,16384]{1,0:T(8,128)(2,1)} %tiles.1, s32[1,256]{1,0:T(1,128)} %expo_in.1, bf16[32,64]{1,0:T(8,128)(2,1)} %rhs_in.1, s32[1,64]{1,0:T(1,128)} %bitcast.3, f32[1,64]{1,0:T(1,128)} %bitcast.4, s32[1,32]{1,0:T(1,128)} %bitcast.5), custom_call_target="tpu_custom_call" | custom-call | flops 805306368 | bytes 2097152 | tf_op jit(solution)/shard_map/krylov/pallas_call | solution.py:313
  150.6 1.3 copy.10
  151.9 1.3 copy.11

commit v5 on v4

--- a/solution.py
+++ b/solution.py
@@ -313,8 +313,8 @@
         pl.pallas_call(
             kernel,
             out_shape=(
-                jax.ShapeDtypeStruct((32, KEEP), BF16),
-                jax.ShapeDtypeStruct((STEPS, 32), F32),
+                pltpu.VMEM((32, KEEP), BF16),
+                pltpu.VMEM((STEPS, 32), F32),
             ),
             in_specs=[pl.BlockSpec(memory_space=pltpu.HBM)] * 6,
             out_specs=(vmem, vmem),

time: 153 us -> 152 us (level)
  no operation moved by 1% of the time
where the time goes in v5:
time: 152 us
  Pallas kernels  150 us (99%)
    pallas_call x1, Pallas kernels, on_device(): pl.pallas_call(kernel, out_shape=(pltpu.VMEM((32, KEEP), BF16), pltpu.VME...  150 us

profile of v5, /device:TPU:1, one launch (start us, length us, event | category | flops | bytes accessed | tf_op | source)
XLA Modules:
  0.0 151.7 jit_solution(13923429345175419849)
XLA Ops:
  0.6 149.8 %krylov.1 = (bf16[32,64]{1,0:T(8,128)(2,1)S(1)}, f32[12,32]{1,0:T(8,128)S(1)}) custom-call(bf16[64,16384]{1,0:T(8,128)(2,1)} %tiles.1, s32[1,256]{1,0:T(1,128)} %expo_in.1, bf16[32,64]{1,0:T(8,128)(2,1)} %rhs_in.1, s32[1,64]{1,0:T(1,128)} %bitcast.3, f32[1,64]{1,0:T(1,128)} %bitcast.4, s32[1,32]{1,0:T(1,128)} %bitcast.5), custom_call_target="tpu_custom_call" | custom-call | flops 805306368 | bytes 2097152 | tf_op jit(solution)/shard_map/krylov/pallas_call | solution.py:313
  150.5 0.6 copy.10
  151.1 0.6 copy.11

commit v6 on v5

--- a/solution.py
+++ b/solution.py
@@ -204,14 +204,14 @@
 
     def product(step, par):
         blocks(recv.at[par], par, DUE).wait()
-        sums = [jnp.zeros((HALF, ROWS), F32) for _ in range(4)]
+        sums = [jnp.zeros((HALF, ROWS), F32) for _ in range(8)]
         for b in range(CHIPS):
             value = vbuf[par, b].astype(F32)
-            sums[b % 4] += value * value
-        squares = jnp.sum((sums[0] + sums[1]) + (sums[2] + sums[3]), axis=1, keepdims=True)
-        root = jnp.sqrt(squares / ALL + 1e-06)
-        history[core] = jnp.where(lane == step - 1, root, history[core])
-        shrink = jnp.exp2(-jnp.floor(jnp.log2(root))).astype(BF16).astype(F32)
+            sums[b % 8] += value * value
+        squares = jnp.sum(((sums[0] + sums[1]) + (sums[2] + sums[3])) + ((sums[4] + sums[5]) + (sums[6] + sums[7])), axis=1, keepdims=True)
+        mean = squares / ALL + 1e-06
+        shrink = jnp.exp2(-jnp.floor(0.5 * jnp.log2(mean))).astype(BF16).astype(F32)
+        root = jnp.sqrt(mean)
         inverse = 1.0 / root
         spread16 = jnp.broadcast_to(shrink, (HALF, ROWS)).astype(BF16)
         total = jnp.zeros((HALF, ROWS), F32)
@@ -224,6 +224,7 @@
                 part, amat[g * group * ROWS : (g + 1) * group * ROWS, :],
                 (((1,), (0,)), ((), ())), preferred_element_type=F32,
             )
+        history[core] = jnp.where(lane == step - 1, root, history[core])
         own = vbuf[par, base].astype(F32)
         return total * (inverse / shrink) + diag * (own * inverse)
 

time: 152 us -> 152 us (level)
  no operation moved by 1% of the time
where the time goes in v6:
time: 152 us
  Pallas kernels  150 us (99%)
    pallas_call x1, Pallas kernels, on_device(): pl.pallas_call(kernel, out_shape=(pltpu.VMEM((32, KEEP), BF16), pltpu.VME...  150 us

profile of v6, /device:TPU:1, one launch (start us, length us, event | category | flops | bytes accessed | tf_op | source)
XLA Modules:
  0.0 151.8 jit_solution(4035294494298798298)
XLA Ops:
  0.6 149.9 %krylov.1 = (bf16[32,64]{1,0:T(8,128)(2,1)S(1)}, f32[12,32]{1,0:T(8,128)S(1)}) custom-call(bf16[64,16384]{1,0:T(8,128)(2,1)} %tiles.1, s32[1,256]{1,0:T(1,128)} %expo_in.1, bf16[32,64]{1,0:T(8,128)(2,1)} %rhs_in.1, s32[1,64]{1,0:T(1,128)} %bitcast.3, f32[1,64]{1,0:T(1,128)} %bitcast.4, s32[1,32]{1,0:T(1,128)} %bitcast.5), custom_call_target="tpu_custom_call" | custom-call | flops 805306368 | bytes 2097152 | tf_op jit(solution)/shard_map/krylov/pallas_call | solution.py:314
  150.6 0.6 copy.10
  151.2 0.6 copy.11
